TPU v7x, 32 devices: a whole 2x2x4 slice. The times are simulated.
32 devices in a mesh: parts: 2 (over x), lag: 8 (over z, y), row: 2 (over core).
Axes of the slice: x: 2, y: 2, z: 4, core: 2. Of those that a mesh axis runs over, the one named last changes fastest.
Arguments:
- history: bfloat16 [16, 32, 64, 256], P('lag', None, 'parts'), parts along dimension 2, may hold values from -6 to 6
- blocks: bfloat16 [8, 2, 112, 256, 256], P('lag', 'row'), may hold values from -0.0234375 to 0.0234375
- block_row: int32 [8, 2, 112], P('lag', 'row'), may hold values from 0 to 15
- block_source: int32 [8, 2, 112], P('lag', 'row'), may hold values from 0 to 31
- block_lag: int32 [8, 2, 112], P('lag', 'row'), may hold values from 0 to 1
- block_count: int32 [8, 2], P('lag', 'row'), may hold values from 56 to 112, as said below
- cluster_perm: int32 [32], replicated, may hold values from 0 to 31, each once
- self_inverse: bfloat16 [32, 256, 256], P('row'), may hold values from -0.375 to 0.375
- pattern: bfloat16 [32, 64, 256], P('row', 'parts'), parts along dimension 1, may hold values from -6 to 6
- waveform: float32 [12, 64], P(None, 'parts'), parts along dimension 1, may hold values from -5 to 5
Outputs:
- new_history: bfloat16 [16, 32, 64, 256], P('lag', None, 'parts'), parts along dimension 2
There are 2 independent parts, one for each index of `parts`. A program takes and returns all parts, laid end to end along the dimension named above; an argument that names none is the same for every part. Nothing has to cross between parts.
Inputs may be any that keep to these rules, and one draw needn't show every extreme that they name: `block_count`: at least half of each device's blocks are used; some device uses all 112.
All inputs are finite; a program needn't handle non-finite values.
Results may differ from a plain program's by a relative error of at most 0.0075.
Values may be sent and summed in bfloat16 or wider, within the bound.
A program may use at most 64 MiB of HBM per device.

v0:
```python
import functools

import jax
import jax.numpy as jnp
from jax import lax
from jax.experimental import pallas as pl
from jax.experimental.pallas import tpu as pltpu
from jax.sharding import PartitionSpec as P

MESH = pl.DeviceIdType.MESH
UNROLL = 8
CHUNK = 4


def plan(block_row, block_source, block_lag, block_count, cluster_perm, rows):
    clusters = cluster_perm.shape[0]
    sources = block_source.reshape(-1)
    count = sources.shape[0]
    lag = block_lag.reshape(-1)
    number = jnp.arange(count, dtype=jnp.int32)
    matches = sources[:, None] == jnp.arange(clusters, dtype=jnp.int32)[None, :]
    storage = jnp.sum(jnp.where(matches, cluster_perm[None, :], 0), axis=1)
    owner = jnp.where(number < block_count.reshape(()), block_row.reshape(-1), rows)
    key = owner * count + number
    rank = jnp.sum((key[None, :] < key[:, None]).astype(jnp.int32), axis=1)
    chosen = rank[None, :] == number[:, None]

    def ordered(values):
        return jnp.sum(jnp.where(chosen, values[None, :], 0), axis=1)

    sorted_owner = ordered(owner)
    even = ordered(((lag + 1) % 2) * clusters + storage)
    odd = ordered((lag % 2) * clusters + storage)
    keep = (
        jnp.concatenate([jnp.full((1,), -1, jnp.int32), sorted_owner[:-1]]) == sorted_owner
    ).astype(jnp.float32)
    members = owner[None, :] == jnp.arange(rows, dtype=jnp.int32)[:, None]
    below = owner[None, :] <= jnp.arange(rows, dtype=jnp.int32)[:, None]
    end = jnp.maximum(jnp.sum(below.astype(jnp.int32), axis=1) - 1, 0)
    filled = jnp.any(members, axis=1).astype(jnp.float32)
    index = jnp.concatenate([ordered(number), even, odd, end])
    return index, jnp.concatenate([keep, filled])


def kernel(
    shards, steps, index, scale, hist, blocks, inverse, pattern, wave, out,
    state, running, entries, child_odd, child_even, outgoing,
    own_recv, sib_recv, odd_recv, even_recv, sib_send, near_send, far_send, sum_send,
):
    count = blocks.shape[0]
    rows, width, depth = pattern.shape
    clusters = hist.shape[1]
    last = steps + 1
    l = lax.axis_index("lag")
    r = lax.axis_index("row")
    even = lax.rem(l, 2) == 0
    half = pl.ds(r * rows, rows)
    sibling = {"row": 1 - r}

    def lag(distance):
        return {"lag": l + distance}

    has_near = l + 1 < shards
    has_far = jnp.logical_and(even, l + 2 < shards)

    barrier = pltpu.get_barrier_semaphore()

    def greet(device):
        pl.semaphore_signal(barrier, inc=1, device_id=device, device_id_type=MESH)

    greet(sibling)
    pl.when(has_near)(lambda: greet(lag(1)))
    pl.when(l >= 1)(lambda: greet(lag(-1)))
    pl.when(has_far)(lambda: greet(lag(2)))
    back = jnp.logical_and(even, l >= 2)
    pl.when(back)(lambda: greet(lag(-2)))
    total = 1
    for flag in (has_near, l >= 1, has_far, back):
        total = total + flag.astype(jnp.int32)
    pl.semaphore_wait(barrier, total)

    def remote(src, dst, send, recv, device):
        return pltpu.make_async_remote_copy(
            src_ref=src, dst_ref=dst, send_sem=send, recv_sem=recv,
            device_id=device, device_id_type=MESH,
        )

    def near(i, src):
        return remote(src, entries.at[i + 2, half], near_send.at[i], own_recv.at[i + 2], lag(1))

    def far(i, src):
        return remote(src, entries.at[i + 4, half], far_send.at[i], own_recv.at[i + 4], lag(2))

    def across(i):
        here = entries.at[i, half]
        return remote(here, here, sib_send.at[i], sib_recv.at[i], sibling)

    def own(i):
        return entries.at[i, half]

    def sum_down(n):
        return (
            remote(outgoing.at[n], child_odd.at[n], sum_send.at[n], odd_recv.at[n], lag(-1)),
            remote(outgoing.at[n], child_even.at[n], sum_send.at[n], even_recv.at[n], lag(-2)),
        )

    for i in range(2):
        pl.when(has_near)(lambda: near(i, hist.at[1 - i, half]).start())
        pl.when(has_far)(lambda: far(i, hist.at[1 - i, half]).start())
        state[i * clusters : (i + 1) * clusters] = hist[1 - i]

    def acquire(i):
        @pl.when(l >= 1)
        def _():
            pltpu.make_async_copy(own(i), own(i), own_recv.at[i]).wait()
            across(i).start()

        pl.when(jnp.logical_and(jnp.logical_and(even, has_near), i + 2 <= last))(
            lambda: near(i, own(i)).start()
        )
        pl.when(jnp.logical_and(has_far, i + 4 <= last))(lambda: far(i, own(i)).start())
        across(i).wait_recv()

    def step(n, carry):
        @pl.when(n >= 1)
        def _():
            acquire(n + 1)
            slot = lax.rem(n + 1, 2) * clusters

            def move(c, _):
                state[slot + c] = entries[n + 1, c]
                return 0

            lax.fori_loop(0, clusters, move, 0)

        places = count + lax.rem(n, 2) * count

        def group(g, held):
            for u in range(UNROLL):
                b = g * UNROLL + u
                product = lax.dot_general(
                    state[index[places + b]], blocks[index[b]], (((1,), (1,)), ((), ())),
                    preferred_element_type=jnp.float32,
                )
                held = held * scale[b] + product
                running[b] = held
            return held

        lax.fori_loop(0, count // UNROLL, group, jnp.zeros((width, depth), jnp.float32))

        def partial(c):
            return running[index[3 * count + c]] * scale[count + c]

        pl.when(jnp.logical_and(even, has_near))(
            lambda: pltpu.make_async_copy(child_odd.at[n], child_odd.at[n], odd_recv.at[n]).wait()
        )
        pl.when(has_far)(
            lambda: pltpu.make_async_copy(child_even.at[n], child_even.at[n], even_recv.at[n]).wait()
        )

        @pl.when(l == 0)
        def _():
            def solve(g, _):
                for u in range(CHUNK):
                    c = g * CHUNK + u
                    lagsum = partial(c) + child_odd[n, c].astype(jnp.float32)
                    if shards > 2:
                        lagsum = lagsum + child_even[n, c].astype(jnp.float32)
                    driven = wave[n] * pattern[c].astype(jnp.float32) - lagsum
                    solved = lax.dot_general(
                        driven.astype(jnp.bfloat16), inverse[c], (((1,), (1,)), ((), ())),
                        preferred_element_type=jnp.float32,
                    )
                    entries[n + 2, r * rows + c] = solved.astype(jnp.bfloat16)
                piece = entries.at[n + 2, pl.ds(r * rows + g * CHUNK, CHUNK)]
                remote(piece, piece, sib_send.at[n + 2], sib_recv.at[n + 2], sibling).start()
                return 0

            lax.fori_loop(0, rows // CHUNK, solve, 0)

        def collect(terms):
            def one(c, _):
                value = partial(c)
                for term in terms:
                    value = value + term[n, c].astype(jnp.float32)
                outgoing[n, c] = value.astype(jnp.bfloat16)
                return 0

            lax.fori_loop(0, rows, one, 0)

        @pl.when(jnp.logical_not(even))
        def _():
            collect(())
            sum_down(n)[0].start()

        @pl.when(back)
        def _():
            pl.when(has_far)(lambda: collect((child_odd, child_even)))
            pl.when(jnp.logical_not(has_far))(lambda: collect((child_odd,)))
            sum_down(n)[1].start()

        return carry

    lax.fori_loop(0, steps, step, 0)
    acquire(last)
    out[0] = entries[last]
    out[1] = entries[last - 1]

    def drain(i, carry):
        pl.when(i >= 2)(lambda: across(i).wait_send())
        pl.when(
            jnp.logical_and(has_near, jnp.logical_or(i < 2, jnp.logical_and(even, i + 2 <= last)))
        )(lambda: near(i, own(i)).wait_send())
        pl.when(jnp.logical_and(has_far, i + 4 <= last))(lambda: far(i, own(i)).wait_send())
        pl.when(jnp.logical_and(l >= 1, i < steps))(lambda: sum_down(i)[0].wait_send())
        return carry

    lax.fori_loop(0, last + 1, drain, 0)


def body(
    shards,
    history,
    blocks,
    block_row,
    block_source,
    block_lag,
    block_count,
    cluster_perm,
    self_inverse,
    pattern,
    waveform,
):
    rows, width, depth = pattern.shape
    steps = waveform.shape[0]
    lags, clusters = history.shape[:2]
    matrices = blocks.reshape(blocks.shape[2:])
    count = matrices.shape[0]
    index, scale = plan(block_row, block_source, block_lag, block_count, cluster_perm, rows)
    wave = jnp.broadcast_to(waveform[:, :, None], (steps, width, depth))
    vmem = pl.BlockSpec(memory_space=pltpu.VMEM)
    smem = pl.BlockSpec(memory_space=pltpu.SMEM)
    slots = steps + lags
    return pl.pallas_call(
        functools.partial(kernel, shards, steps),
        out_shape=jax.ShapeDtypeStruct(history.shape, history.dtype),
        in_specs=[smem, smem] + [vmem] * 5,
        out_specs=vmem,
        scratch_shapes=[
            pltpu.VMEM((lags * clusters, width, depth), jnp.bfloat16),
            pltpu.VMEM((count, width, depth), jnp.float32),
            pltpu.VMEM((slots, clusters, width, depth), jnp.bfloat16),
            pltpu.VMEM((steps, rows, width, depth), jnp.bfloat16),
            pltpu.VMEM((steps, rows, width, depth), jnp.bfloat16),
            pltpu.VMEM((steps, rows, width, depth), jnp.bfloat16),
            pltpu.SemaphoreType.DMA((slots,)),
            pltpu.SemaphoreType.DMA((slots,)),
            pltpu.SemaphoreType.DMA((steps,)),
            pltpu.SemaphoreType.DMA((steps,)),
            pltpu.SemaphoreType.DMA((slots,)),
            pltpu.SemaphoreType.DMA((slots,)),
            pltpu.SemaphoreType.DMA((slots,)),
            pltpu.SemaphoreType.DMA((steps,)),
        ],
        compiler_params=pltpu.CompilerParams(
            collective_id=0, has_side_effects=True, vmem_limit_bytes=58 * 1024 * 1024
        ),
        name="march",
    )(index, scale, history, matrices, self_inverse, pattern, wave)


def solution(mesh):
    in_specs = (
        P("lag", None, "parts", None),
        P("lag", "row", None, None, None),
        P("lag", "row", None),
        P("lag", "row", None),
        P("lag", "row", None),
        P("lag", "row"),
        P(),
        P("row", None, None),
        P("row", "parts", None),
        P(None, "parts"),
    )
    out_specs = P("lag", None, "parts", None)
    return jax.shard_map(
        functools.partial(body, mesh.shape["lag"]), mesh=mesh, in_specs=in_specs,
        out_specs=out_specs, check_vma=False,
    )
```

profile of v0, /device:TPU:1, one launch (start us, length us, event | category | flops | bytes accessed | tf_op | source)
XLA Modules:
  0.0 153.3 jit_solution(12178232297435657649)
XLA Ops:
  0.7 0.8 select_reduce_fusion.4
  1.4 0.7 fusion.2
  2.1 0.2 convert_reduce_fusion
  2.3 0.1 convert_reduce_fusion.1
  2.4 0.1 fusion
  2.5 0.2 select_reduce_fusion
  2.7 0.7 pad_add_fusion.index
  3.3 0.1 add_compare_fusion
  3.4 0.6 add_convert_fusion.scale
  4.0 1.6 %broadcast_in_dim.74.wave = f32[12,32,256]{2,1,0:T(8,128)} broadcast(f32[12,32]{1,0:T(8,128)} %param.19), dimensions={0,1} | broadcast | bytes 394752 | tf_op jit(solution)/shard_map/broadcast_in_dim | solution.py:240
  5.6 145.4 %march.1 = bf16[2,32,32,256]{3,2,1,0:T(8,128)(2,1)} custom-call(s32[352]{0:T(512)} %pad_add_fusion.index, f32[128]{0:T(128)} %add_convert_fusion.scale, bf16[2,32,32,256]{3,2,1,0:T(8,128)(2,1)} %hist.1, bf16[112,256,256]{2,1,0:T(8,128)(2,1)} %bitcast.13, bf16[16,256,256]{2,1,0:T(8,128)(2,1)} %inverse.1, bf16[16,32,256]{2,1,0:T(8,128)(2,1)} %pattern.1, ...), custom_call_target="tpu_custom_call" | custom-call | tf_op jit(solution)/shard_map/march/pallas_call | solution.py:244
  151.0 2.3 %copy.13 = bf16[2,32,32,256]{3,2,1,0:T(8,128)(2,1)} copy(bf16[2,32,32,256]{3,2,1,0:T(8,128)(2,1)} %march.1) | data formatting | bytes 2097152
  (1 shorter events, 0.0 us)
where the time goes:
time: 154 us; the launch traced here: 153 us
  Pallas kernels  145 us (94%)
  local copies, waits for them, and re-layouts  3.82 us (2%)
  other arithmetic  3.34 us (2%)
    pallas_call x1, Pallas kernels, body(): pl.pallas_call(functools.partial(kernel, shards, steps), out_shape=jax.Sh...  145 us

commit v1 on v0

--- a/solution.py
+++ b/solution.py
@@ -8,7 +8,7 @@
 from jax.sharding import PartitionSpec as P
 
 MESH = pl.DeviceIdType.MESH
-UNROLL = 8
+UNROLL = 28
 CHUNK = 4
 
 
@@ -98,33 +98,57 @@
     def own(i):
         return entries.at[i, half]
 
-    def sum_down(n):
+    def sum_down(n, g):
+        src = outgoing.at[n, pl.ds(g * CHUNK, CHUNK)]
+        sem = sum_send.at[n]
+        part = pl.ds(g * CHUNK, CHUNK)
         return (
-            remote(outgoing.at[n], child_odd.at[n], sum_send.at[n], odd_recv.at[n], lag(-1)),
-            remote(outgoing.at[n], child_even.at[n], sum_send.at[n], even_recv.at[n], lag(-2)),
-        )
+            lambda: remote(src, child_odd.at[n, part], sem, odd_recv.at[n, g], lag(-1)),
+            lambda: remote(src, child_even.at[n, part], sem, even_recv.at[n, g], lag(-2)),
+        )
+
+    def await_sums(n, g):
+        part = pl.ds(g * CHUNK, CHUNK)
+
+        @pl.when(jnp.logical_and(even, has_near))
+        def _():
+            ref = child_odd.at[n, part]
+            pltpu.make_async_copy(ref, ref, odd_recv.at[n, g]).wait()
+
+        @pl.when(has_far)
+        def _():
+            ref = child_even.at[n, part]
+            pltpu.make_async_copy(ref, ref, even_recv.at[n, g]).wait()
 
     for i in range(2):
         pl.when(has_near)(lambda: near(i, hist.at[1 - i, half]).start())
-        pl.when(has_far)(lambda: far(i, hist.at[1 - i, half]).start())
         state[i * clusters : (i + 1) * clusters] = hist[1 - i]
 
-    def acquire(i):
+    def relay(i):
         @pl.when(l >= 1)
         def _():
             pltpu.make_async_copy(own(i), own(i), own_recv.at[i]).wait()
             across(i).start()
 
-        pl.when(jnp.logical_and(jnp.logical_and(even, has_near), i + 2 <= last))(
+        pl.when(jnp.logical_and(jnp.logical_and(back, has_near), i + 2 <= last))(
             lambda: near(i, own(i)).start()
         )
-        pl.when(jnp.logical_and(has_far, i + 4 <= last))(lambda: far(i, own(i)).start())
-        across(i).wait_recv()
+        pl.when(jnp.logical_and(jnp.logical_and(back, has_far), i + 4 <= last))(
+            lambda: far(i, own(i)).start()
+        )
 
     def step(n, carry):
         @pl.when(n >= 1)
         def _():
-            acquire(n + 1)
+            @pl.when(n == 1)
+            def _():
+                for i in range(2):
+                    pl.when(has_far)(lambda: far(i, hist.at[1 - i, half]).start())
+                pl.when(back)(lambda: relay(2))
+
+            pl.when(back)(lambda: relay(n + 2))
+            pl.when(jnp.logical_not(back))(lambda: relay(n + 1))
+            across(n + 1).wait_recv()
             slot = lax.rem(n + 1, 2) * clusters
 
             def move(c, _):
@@ -151,22 +175,19 @@
         def partial(c):
             return running[index[3 * count + c]] * scale[count + c]
 
-        pl.when(jnp.logical_and(even, has_near))(
-            lambda: pltpu.make_async_copy(child_odd.at[n], child_odd.at[n], odd_recv.at[n]).wait()
-        )
-        pl.when(has_far)(
-            lambda: pltpu.make_async_copy(child_even.at[n], child_even.at[n], even_recv.at[n]).wait()
-        )
-
         @pl.when(l == 0)
         def _():
+            width_steps = lax.broadcasted_iota(jnp.int32, wave.shape, 1)
+            drive = jnp.sum(jnp.where(width_steps == n, wave[...], 0.0), axis=1, keepdims=True)
+
             def solve(g, _):
+                await_sums(n, g)
                 for u in range(CHUNK):
                     c = g * CHUNK + u
                     lagsum = partial(c) + child_odd[n, c].astype(jnp.float32)
                     if shards > 2:
                         lagsum = lagsum + child_even[n, c].astype(jnp.float32)
-                    driven = wave[n] * pattern[c].astype(jnp.float32) - lagsum
+                    driven = drive * pattern[c].astype(jnp.float32) - lagsum
                     solved = lax.dot_general(
                         driven.astype(jnp.bfloat16), inverse[c], (((1,), (1,)), ((), ())),
                         preferred_element_type=jnp.float32,
@@ -174,35 +195,55 @@
                     entries[n + 2, r * rows + c] = solved.astype(jnp.bfloat16)
                 piece = entries.at[n + 2, pl.ds(r * rows + g * CHUNK, CHUNK)]
                 remote(piece, piece, sib_send.at[n + 2], sib_recv.at[n + 2], sibling).start()
+                if shards > 1:
+
+                    @pl.when(n + 4 <= last)
+                    def _():
+                        there = entries.at[n + 4, pl.ds(r * rows + g * CHUNK, CHUNK)]
+                        remote(
+                            piece, there, near_send.at[n + 2], own_recv.at[n + 4], lag(1)
+                        ).start()
+
+                if shards > 2:
+
+                    @pl.when(n + 6 <= last)
+                    def _():
+                        there = entries.at[n + 6, pl.ds(r * rows + g * CHUNK, CHUNK)]
+                        remote(
+                            piece, there, far_send.at[n + 2], own_recv.at[n + 6], lag(2)
+                        ).start()
+
                 return 0
 
             lax.fori_loop(0, rows // CHUNK, solve, 0)
 
-        def collect(terms):
-            def one(c, _):
-                value = partial(c)
-                for term in terms:
-                    value = value + term[n, c].astype(jnp.float32)
-                outgoing[n, c] = value.astype(jnp.bfloat16)
+        def collect(terms, target):
+            def piece(g, _):
+                if terms:
+                    await_sums(n, g)
+                for u in range(CHUNK):
+                    c = g * CHUNK + u
+                    value = partial(c)
+                    for term in terms:
+                        value = value + term[n, c].astype(jnp.float32)
+                    outgoing[n, c] = value.astype(jnp.bfloat16)
+                sum_down(n, g)[target]().start()
                 return 0
 
-            lax.fori_loop(0, rows, one, 0)
-
-        @pl.when(jnp.logical_not(even))
-        def _():
-            collect(())
-            sum_down(n)[0].start()
+            lax.fori_loop(0, rows // CHUNK, piece, 0)
+
+        pl.when(jnp.logical_not(even))(lambda: collect((), 0))
 
         @pl.when(back)
         def _():
-            pl.when(has_far)(lambda: collect((child_odd, child_even)))
-            pl.when(jnp.logical_not(has_far))(lambda: collect((child_odd,)))
-            sum_down(n)[1].start()
+            pl.when(has_far)(lambda: collect((child_odd, child_even), 1))
+            pl.when(jnp.logical_not(has_far))(lambda: collect((child_odd,), 1))
 
         return carry
 
     lax.fori_loop(0, steps, step, 0)
-    acquire(last)
+    pl.when(jnp.logical_not(back))(lambda: relay(last))
+    across(last).wait_recv()
     out[0] = entries[last]
     out[1] = entries[last - 1]
 
@@ -212,7 +253,10 @@
             jnp.logical_and(has_near, jnp.logical_or(i < 2, jnp.logical_and(even, i + 2 <= last)))
         )(lambda: near(i, own(i)).wait_send())
         pl.when(jnp.logical_and(has_far, i + 4 <= last))(lambda: far(i, own(i)).wait_send())
-        pl.when(jnp.logical_and(l >= 1, i < steps))(lambda: sum_down(i)[0].wait_send())
+        whole = outgoing.at[i]
+        pl.when(jnp.logical_and(l >= 1, i < steps))(
+            lambda: pltpu.make_async_copy(whole, whole, sum_send.at[i]).wait()
+        )
         return carry
 
     lax.fori_loop(0, last + 1, drain, 0)
@@ -237,7 +281,7 @@
     matrices = blocks.reshape(blocks.shape[2:])
     count = matrices.shape[0]
     index, scale = plan(block_row, block_source, block_lag, block_count, cluster_perm, rows)
-    wave = jnp.broadcast_to(waveform[:, :, None], (steps, width, depth))
+    wave = waveform.T
     vmem = pl.BlockSpec(memory_space=pltpu.VMEM)
     smem = pl.BlockSpec(memory_space=pltpu.SMEM)
     slots = steps + lags
@@ -255,8 +299,8 @@
             pltpu.VMEM((steps, rows, width, depth), jnp.bfloat16),
             pltpu.SemaphoreType.DMA((slots,)),
             pltpu.SemaphoreType.DMA((slots,)),
-            pltpu.SemaphoreType.DMA((steps,)),
-            pltpu.SemaphoreType.DMA((steps,)),
+            pltpu.SemaphoreType.DMA((steps, rows // CHUNK)),
+            pltpu.SemaphoreType.DMA((steps, rows // CHUNK)),
             pltpu.SemaphoreType.DMA((slots,)),
             pltpu.SemaphoreType.DMA((slots,)),
             pltpu.SemaphoreType.DMA((slots,)),

time: 154 us -> 137 us (0.89)
  Pallas kernels: 145 us -> 129 us
    pallas_call x1, Pallas kernels: 145 us -> 129 us  [body(): pl.pallas_call(functools.partial(kernel, shards, steps), out_shape=jax.Sh...]
    broadcast_in_dim x1 -> x0, local copies, waits for them, and re-layouts: 1.56 us -> none  [body(): wave = jnp.broadcast_to(waveform[:, :, None], (steps, width, depth))]
    unnamed x1 -> x2, local copies, waits for them, and re-layouts: 2.26 us -> 3.64 us
where the time goes in v1:
time: 137 us; the launch traced here: 136 us
  Pallas kernels  129 us (94%)
  local copies, waits for them, and re-layouts  3.64 us (3%)
  other arithmetic  3.34 us (2%)
    pallas_call x1, Pallas kernels, body(): pl.pallas_call(functools.partial(kernel, shards, steps), out_shape=jax.Sh...  129 us
    unnamed x2, local copies, waits for them, and re-layouts  3.64 us

profile of v1, /device:TPU:1, one launch (start us, length us, event | category | flops | bytes accessed | tf_op | source)
XLA Modules:
  0.0 136.4 jit_solution(6082477932675172463)
XLA Ops:
  0.7 0.8 select_reduce_fusion.4
  1.4 0.7 fusion.2
  2.1 0.2 convert_reduce_fusion
  2.3 0.1 convert_reduce_fusion.1
  2.4 0.1 fusion
  2.5 0.2 select_reduce_fusion
  2.7 0.7 pad_add_fusion.index
  3.3 0.1 add_compare_fusion
  3.4 0.6 add_convert_fusion.scale
  4.0 1.4 %copy.12 = f32[12,32]{0,1:T(8,128)} copy(f32[12,32]{1,0:T(8,128)} %param.19) | data formatting | bytes 3072 | tf_op args[9]
  5.4 128.7 %march.1 = bf16[2,32,32,256]{3,2,1,0:T(8,128)(2,1)} custom-call(s32[352]{0:T(512)} %pad_add_fusion.index, f32[128]{0:T(128)} %add_convert_fusion.scale, bf16[2,32,32,256]{3,2,1,0:T(8,128)(2,1)} %hist.1, bf16[112,256,256]{2,1,0:T(8,128)(2,1)} %bitcast.14, bf16[16,256,256]{2,1,0:T(8,128)(2,1)} %inverse.1, bf16[16,32,256]{2,1,0:T(8,128)(2,1)} %pattern.1, ...), custom_call_target="tpu_custom_call" | custom-call | tf_op jit(solution)/shard_map/march/pallas_call | solution.py:288
  134.1 2.3 %copy.15 = bf16[2,32,32,256]{3,2,1,0:T(8,128)(2,1)} copy(bf16[2,32,32,256]{3,2,1,0:T(8,128)(2,1)} %march.1) | data formatting | bytes 2097152
  (1 shorter events, 0.0 us)

commit v2 on v1

--- a/solution.py
+++ b/solution.py
@@ -44,7 +44,7 @@
 
 def kernel(
     shards, steps, index, scale, hist, blocks, inverse, pattern, wave, out,
-    state, running, entries, child_odd, child_even, outgoing,
+    state, running, flipped, flipped_inverse, entries, child_odd, child_even, outgoing,
     own_recv, sib_recv, odd_recv, even_recv, sib_send, near_send, far_send, sum_send,
 ):
     count = blocks.shape[0]
@@ -159,18 +159,35 @@
 
         places = count + lax.rem(n, 2) * count
 
-        def group(g, held):
+        def group(first, g, held):
             for u in range(UNROLL):
                 b = g * UNROLL + u
-                product = lax.dot_general(
-                    state[index[places + b]], blocks[index[b]], (((1,), (1,)), ((), ())),
-                    preferred_element_type=jnp.float32,
+                if first:
+                    turned = blocks[index[b]].T
+                    flipped[b] = turned
+                else:
+                    turned = flipped[b]
+                product = jnp.dot(
+                    state[index[places + b]], turned, preferred_element_type=jnp.float32
                 )
                 held = held * scale[b] + product
                 running[b] = held
             return held
 
-        lax.fori_loop(0, count // UNROLL, group, jnp.zeros((width, depth), jnp.float32))
+        def multiply(first):
+            zero = jnp.zeros((width, depth), jnp.float32)
+            lax.fori_loop(0, count // UNROLL, functools.partial(group, first), zero)
+
+        pl.when(n == 0)(lambda: multiply(True))
+        pl.when(n > 0)(lambda: multiply(False))
+
+        @pl.when(jnp.logical_and(n == 0, l == 0))
+        def _():
+            def turn(c, _):
+                flipped_inverse[c] = inverse[c].T
+                return 0
+
+            lax.fori_loop(0, rows, turn, 0)
 
         def partial(c):
             return running[index[3 * count + c]] * scale[count + c]
@@ -188,8 +205,8 @@
                     if shards > 2:
                         lagsum = lagsum + child_even[n, c].astype(jnp.float32)
                     driven = drive * pattern[c].astype(jnp.float32) - lagsum
-                    solved = lax.dot_general(
-                        driven.astype(jnp.bfloat16), inverse[c], (((1,), (1,)), ((), ())),
+                    solved = jnp.dot(
+                        driven.astype(jnp.bfloat16), flipped_inverse[c],
                         preferred_element_type=jnp.float32,
                     )
                     entries[n + 2, r * rows + c] = solved.astype(jnp.bfloat16)
@@ -293,6 +310,8 @@
         scratch_shapes=[
             pltpu.VMEM((lags * clusters, width, depth), jnp.bfloat16),
             pltpu.VMEM((count, width, depth), jnp.float32),
+            pltpu.VMEM((count, depth, depth), jnp.bfloat16),
+            pltpu.VMEM((rows, depth, depth), jnp.bfloat16),
             pltpu.VMEM((slots, clusters, width, depth), jnp.bfloat16),
             pltpu.VMEM((steps, rows, width, depth), jnp.bfloat16),
             pltpu.VMEM((steps, rows, width, depth), jnp.bfloat16),
@@ -307,7 +326,7 @@
             pltpu.SemaphoreType.DMA((steps,)),
         ],
         compiler_params=pltpu.CompilerParams(
-            collective_id=0, has_side_effects=True, vmem_limit_bytes=58 * 1024 * 1024
+            collective_id=0, has_side_effects=True, vmem_limit_bytes=60 * 1024 * 1024
         ),
         name="march",
     )(index, scale, history, matrices, self_inverse, pattern, wave)

time: 137 us -> 126 us (0.920)
  Pallas kernels: 129 us -> 118 us
    pallas_call x1, Pallas kernels: 129 us -> 118 us  [body(): pl.pallas_call(functools.partial(kernel, shards, steps), out_shape=jax.Sh...]
where the time goes in v2:
time: 126 us
  Pallas kernels  118 us (94%)
  local copies, waits for them, and re-layouts  3.64 us (3%)
  other arithmetic  3.34 us (3%)
    pallas_call x1, Pallas kernels, body(): pl.pallas_call(functools.partial(kernel, shards, steps), out_shape=jax.Sh...  118 us
    unnamed x2, local copies, waits for them, and re-layouts  3.64 us

profile of v2, /device:TPU:1, one launch (start us, length us, event | category | flops | bytes accessed | tf_op | source)
XLA Modules:
  0.0 125.9 jit_solution(881635617634322378)
XLA Ops:
  0.7 0.8 select_reduce_fusion.4
  1.4 0.7 fusion.2
  2.1 0.2 convert_reduce_fusion
  2.3 0.1 convert_reduce_fusion.1
  2.4 0.1 fusion
  2.5 0.2 select_reduce_fusion
  2.7 0.7 pad_add_fusion.index
  3.3 0.1 add_compare_fusion
  3.4 0.6 add_convert_fusion.scale
  4.0 1.4 %copy.12 = f32[12,32]{0,1:T(8,128)} copy(f32[12,32]{1,0:T(8,128)} %param.19) | data formatting | bytes 3072 | tf_op args[9]
  5.4 118.2 %march.1 = bf16[2,32,32,256]{3,2,1,0:T(8,128)(2,1)} custom-call(s32[352]{0:T(512)} %pad_add_fusion.index, f32[128]{0:T(128)} %add_convert_fusion.scale, bf16[2,32,32,256]{3,2,1,0:T(8,128)(2,1)} %hist.1, bf16[112,256,256]{2,1,0:T(8,128)(2,1)} %bitcast.14, bf16[16,256,256]{2,1,0:T(8,128)(2,1)} %inverse.1, bf16[16,32,256]{2,1,0:T(8,128)(2,1)} %pattern.1, ...), custom_call_target="tpu_custom_call" | custom-call | tf_op jit(solution)/shard_map/march/pallas_call | solution.py:305
  123.6 2.3 %copy.15 = bf16[2,32,32,256]{3,2,1,0:T(8,128)(2,1)} copy(bf16[2,32,32,256]{3,2,1,0:T(8,128)(2,1)} %march.1) | data formatting | bytes 2097152
  (1 shorter events, 0.0 us)

commit v3 on v2

--- a/solution.py
+++ b/solution.py
@@ -8,7 +8,7 @@
 from jax.sharding import PartitionSpec as P
 
 MESH = pl.DeviceIdType.MESH
-UNROLL = 28
+UNROLL = 56
 CHUNK = 4
 
 

time: 126 us -> 125 us (level)
  no operation moved by 1% of the time
where the time goes in v3:
time: 125 us
  Pallas kernels  117 us (94%)
  local copies, waits for them, and re-layouts  3.64 us (3%)
  other arithmetic  3.34 us (3%)
    pallas_call x1, Pallas kernels, body(): pl.pallas_call(functools.partial(kernel, shards, steps), out_shape=jax.Sh...  117 us
    unnamed x2, local copies, waits for them, and re-layouts  3.64 us

profile of v3, /device:TPU:1, one launch (start us, length us, event | category | flops | bytes accessed | tf_op | source)
XLA Modules:
  0.0 124.8 jit_solution(13537399882865669880)
XLA Ops:
  0.7 0.8 select_reduce_fusion.4
  1.4 0.7 fusion.2
  2.1 0.2 convert_reduce_fusion
  2.3 0.1 convert_reduce_fusion.1
  2.4 0.1 fusion
  2.5 0.2 select_reduce_fusion
  2.7 0.7 pad_add_fusion.index
  3.3 0.1 add_compare_fusion
  3.4 0.6 add_convert_fusion.scale
  4.0 1.4 %copy.12 = f32[12,32]{0,1:T(8,128)} copy(f32[12,32]{1,0:T(8,128)} %param.19) | data formatting | bytes 3072 | tf_op args[9]
  5.4 117.1 %march.1 = bf16[2,32,32,256]{3,2,1,0:T(8,128)(2,1)} custom-call(s32[352]{0:T(512)} %pad_add_fusion.index, f32[128]{0:T(128)} %add_convert_fusion.scale, bf16[2,32,32,256]{3,2,1,0:T(8,128)(2,1)} %hist.1, bf16[112,256,256]{2,1,0:T(8,128)(2,1)} %bitcast.14, bf16[16,256,256]{2,1,0:T(8,128)(2,1)} %inverse.1, bf16[16,32,256]{2,1,0:T(8,128)(2,1)} %pattern.1, ...), custom_call_target="tpu_custom_call" | custom-call | tf_op jit(solution)/shard_map/march/pallas_call | solution.py:305
  122.5 2.3 %copy.15 = bf16[2,32,32,256]{3,2,1,0:T(8,128)(2,1)} copy(bf16[2,32,32,256]{3,2,1,0:T(8,128)(2,1)} %march.1) | data formatting | bytes 2097152
  (1 shorter events, 0.0 us)
